TPU v7x, 32 devices: a whole 2x2x4 slice. The times are simulated.
32 devices in a mesh: grp: 2 (over x), seq: 16 (over z, y, core).
Axes of the slice: x: 2, y: 2, z: 4, core: 2. Of those that a mesh axis runs over, the one named last changes fastest.
Arguments:
- tokens: bfloat16 [2, 131072, 768], P('grp', 'seq'), parts along dimension 0, may hold values from -36 to 36
- right_factor: bfloat16 [256, 512, 512], P('seq'), may hold values from -0.25 to 0.25
- left_factor: bfloat16 [512, 256, 256], P('seq'), may hold values from -0.375 to 0.375
- twiddle: float32 [256, 512], P('seq'), may hold values from 0.5 to 2
- norm_gain: float32 [768], replicated, may hold values from 0.1 to 1.9
- mix_gain: float32 [768], replicated, may hold values from 0.1 to 1.9
- value_weight: bfloat16 [768, 768], replicated, may hold values from -0.21875 to 0.21875
- gate_weight: bfloat16 [768, 768], replicated, may hold values from -0.21875 to 0.21875
Outputs:
- layer_out: bfloat16 [2, 131072, 768], P('grp', 'seq'), parts along dimension 0
There are 2 independent parts, one for each index of `grp`. A program takes and returns all parts, laid end to end along the dimension named above; an argument that names none is the same for every part. Nothing has to cross between parts.
All inputs are finite; a program needn't handle non-finite values.
Results may differ from a plain program's by a relative error of at most 0.0051.
Values may be sent and summed in bfloat16 or wider, within the bound.
A program may use at most 192 MiB of HBM per device.

v0:
```python
import jax
import jax.numpy as jnp
from jax import lax
from jax.sharding import PartitionSpec as P


def rms_scale(values, gain):
    mean_square = jnp.mean(values * values, axis=-1, keepdims=True)
    return values * lax.rsqrt(mean_square + 1e-05) * gain


def second_section(columns, left_factor):
    mixed = jnp.einsum("jia,sajc->sijc", left_factor, columns, preferred_element_type=jnp.float32)
    return mixed.astype(jnp.bfloat16)


def body(
    tokens, right_factor, left_factor, twiddle, norm_gain, mix_gain, value_weight, gate_weight
):
    seqs_here, rows_here, width = tokens.shape
    blocks_here = right_factor.shape[0]
    block_len = right_factor.shape[1]
    widened = tokens.astype(jnp.float32)
    normed = rms_scale(widened, norm_gain).astype(jnp.bfloat16)
    blocked = normed.reshape(seqs_here, blocks_here, block_len, width)
    section_one = jnp.einsum(
        "ajb,sabc->sajc", right_factor, blocked, preferred_element_type=jnp.float32
    )
    section_one = (section_one * twiddle[None, :, :, None]).astype(jnp.bfloat16)
    columns = lax.all_to_all(section_one, "seq", split_axis=2, concat_axis=1, tiled=True)
    mixed_cols = second_section(columns, left_factor)
    mixed_back = lax.all_to_all(mixed_cols, "seq", split_axis=1, concat_axis=2, tiled=True)
    residual_sum = widened + mixed_back.reshape(seqs_here, rows_here, width).astype(jnp.float32)
    mix_normed = (
        rms_scale(residual_sum, mix_gain).astype(jnp.bfloat16).reshape(seqs_here * rows_here, width)
    )
    values_out = jnp.dot(mix_normed, value_weight, preferred_element_type=jnp.float32)
    gates = jnp.dot(mix_normed, gate_weight, preferred_element_type=jnp.float32)
    gated = (values_out * jax.nn.sigmoid(gates)).reshape(seqs_here, rows_here, width)
    return (residual_sum + gated).astype(jnp.bfloat16)


def solution(mesh):
    return jax.shard_map(
        body,
        mesh=mesh,
        in_specs=(
            P("grp", "seq", None),
            P("seq", None, None),
            P("seq", None, None),
            P("seq", None),
            P(),
            P(),
            P(),
            P(),
        ),
        out_specs=P("grp", "seq", None),
        check_vma=False,
    )
```

profile of v0, /device:TPU:13, one launch (start us, length us, event | category | flops | bytes accessed | tf_op | source)
XLA Modules:
  0.0 758.1 jit_solution(9899287681793575877)
XLA Ops:
  0.0 0.0 copy-start
  0.0 0.0 copy-start.2
  0.0 7.2 fusion
  7.2 0.0 copy-done.2
  7.3 0.0 copy-start.4
  7.3 11.8 %fusion.2 = bf16[1,8192,768]{2,1,0:T(8,128)(2,1)} fusion(bf16[1,8192,768]{2,1,0:T(8,128)(2,1)} %param.8, f32[768]{0:T(1024)S(1)} %copy-done.2, f32[8192]{0:T(1024)S(1)} %add_rsqrt_fusion.1), kind=kLoop, calls=%fused_computation.5 | loop fusion | flops 25165824 | bytes 25201664 | tf_op jit(solution)/shard_map/convert_element_type | solution.py:24
  19.1 0.0 copy-done.4
  19.1 16.0 %fusion.9 = bf16[1,16,512,768]{2,3,1,0:T(8,128)(2,1)} fusion(f32[16,512]{1,0:T(8,128)S(1)} %copy-done.4, bf16[16,512,768]{2,1,0:T(8,128)(2,1)} %bitcast.45, bf16[16,512,512]{2,1,0:T(8,128)(2,1)} %param.9), kind=kOutput, calls=%fused_computation.15 | convolution fusion | flops 6455033856 | bytes 33587200 | tf_op jit(solution)/shard_map/ajb,sabc->sajc/dot_general | solution.py:26
  35.1 17.6 %copy.19 = bf16[1,16,512,768]{3,1,0,2:T(8,128)(2,1)} copy(bf16[1,16,512,768]{2,3,1,0:T(8,128)(2,1)} %fusion.9) | data formatting | bytes 25165824 | tf_op jit(solution)/shard_map/convert_element_type | solution.py:29
  52.7 278.6 %all_to_all.24 = bf16[1,16,512,768]{3,1,0,2:T(8,128)(2,1)S(1)} all-to-all(bf16[1,16,512,768]{3,1,0,2:T(8,128)(2,1)} %copy.19), channel_id=1, replica_groups=mesh['grp'=2,'seq'=16] {'seq'}, dimensions={2} | all-to-all | bytes 25165824 | tf_op jit(solution)/shard_map/all_to_all | solution.py:30
  331.3 8.8 %copy.20 = bf16[1,16,512,768]{3,2,1,0:T(8,128)(2,1)S(1)} copy(bf16[1,16,512,768]{3,1,0,2:T(8,128)(2,1)S(1)} %all_to_all.24) | data formatting | bytes 25165824 | tf_op jit(solution)/shard_map/all_to_all | solution.py:30
  340.1 5.3 copy.21
  345.4 18.1 %convert_bitcast_fusion.1 = bf16[1,256,32,768]{1,3,2,0:T(8,128)(2,1)} fusion(bf16[32,256,256]{2,1,0:T(8,128)(2,1)} %param.10, bf16[256,32,768]{2,1,0:T(8,128)(2,1)} %bitcast.44), kind=kOutput, calls=%fused_computation.22 | convolution fusion | flops 3227516928 | bytes 29360128 | tf_op jit(solution)/shard_map/jia,sajc->sijc/dot_general | solution.py:13
  363.5 16.6 %copy.23 = bf16[1,256,32,768]{3,2,0,1:T(8,128)(2,1)} copy(bf16[1,256,32,768]{1,3,2,0:T(8,128)(2,1)} %convert_bitcast_fusion.1) | data formatting | bytes 25165824 | tf_op jit(solution)/shard_map/convert_element_type | solution.py:14
  380.1 278.1 %all_to_all.25 = bf16[1,256,32,768]{3,2,0,1:T(8,128)(2,1)S(1)} all-to-all(bf16[1,256,32,768]{3,2,0,1:T(8,128)(2,1)} %copy.23), channel_id=1, replica_groups=mesh['grp'=2,'seq'=16] {'seq'}, dimensions={1} | all-to-all | bytes 25165824 | tf_op jit(solution)/shard_map/all_to_all | solution.py:32
  658.2 0.0 slice-start
  658.2 0.0 slice-start.1
  658.2 10.6 %convert_bitcast_fusion = f32[1,16,16,32,768]{4,3,1,2,0:T(8,128)} fusion(bf16[1,16,16,32,768]{4,3,2,1,0:T(8,128)(2,1)S(1)} %bitcast.43), kind=kLoop, calls=%fused_computation.6 | loop fusion | flops 6291456 | bytes 37748736 | tf_op jit(solution)/shard_map/convert_element_type | solution.py:33
  668.8 0.0 slice-start.2
  668.8 18.3 %copy.25 = f32[1,16,16,32,768]{4,3,2,1,0:T(8,128)} copy(f32[1,16,16,32,768]{4,3,1,2,0:T(8,128)} %convert_bitcast_fusion) | data formatting | bytes 50331648 | tf_op jit(solution)/shard_map/convert_element_type | solution.py:33
  687.1 0.0 slice-done
  687.1 0.0 slice-done.1
  687.1 0.0 slice-done.2
  687.1 0.0 copy-start.5
  687.1 17.8 %multiply_reduce_fusion = (f32[8192]{0:T(1024)S(1)}, f32[1,8192,768]{2,1,0:T(8,128)}) fusion(f32[1,16,16,32,768]{4,3,2,1,0:T(8,128)} %copy.25, bf16[1,8192,768]{2,1,0:T(8,128)(2,1)S(1)} %bitcast.41), kind=kLoop, calls=%fused_computation.12 | loop fusion | flops 25157632 | bytes 62947328 | tf_op jit(solution)/shard_map/reduce_sum | solution.py:8
  704.9 0.0 copy-done
  704.9 0.0 copy-done.5
  705.0 0.0 copy-start.3
  705.0 19.5 %fusion.7 = f32[8192,768]{1,0:T(8,128)} fusion(bf16[768,768]{1,0:T(8,128)(2,1)S(1)} %copy-done, f32[1,8192,768]{2,1,0:T(8,128)} %get-tuple-element.6, f32[768]{0:T(1024)S(1)} %copy-done.5, f32[8192]{0:T(1024)S(1)} %add_rsqrt_fusion), kind=kOutput, calls=%fused_computation.14 | convolution fusion | flops 9682550784 | bytes 51547136 | tf_op jit(solution)/shard_map/dot_general | solution.py:37
  724.4 0.0 copy-done.3
  724.4 0.0 copy-start.1
  724.4 33.6 %fusion.3 = bf16[1,8192,768]{2,1,0:T(8,128)(2,1)} fusion(f32[1,8192,768]{2,1,0:T(8,128)} %get-tuple-element.6, f32[8192,768]{1,0:T(8,128)} %fusion.7, bf16[768,768]{1,0:T(8,128)(2,1)S(1)} %copy-done.3, f32[768]{0:T(1024)S(1)} %copy-done.5, f32[8192]{0:T(1024)S(1)} %add_rsqrt_fusion), kind=kOutput, calls=%fused_computation.8 | convolution fusion | flops 9720299520 | bytes 64130048 | tf_op jit(solution)/shard_map/dot_general | solution.py:38
  758.1 0.0 copy-done.1
  (3 shorter events, 0.0 us)
Async XLA Ops:
  0.0 704.9 %copy-start = (bf16[768,768]{1,0:T(8,128)(2,1)S(1)}, bf16[768,768]{1,0:T(8,128)(2,1)}, u32[]{:S(2)}) copy-start(bf16[768,768]{1,0:T(8,128)(2,1)} %param.14) | copy-start | bytes 3538948
  0.0 7.2 copy-start.2
  7.3 11.8 %copy-start.4 = (f32[16,512]{1,0:T(8,128)S(1)}, f32[16,512]{1,0:T(8,128)}, u32[]{:S(2)}) copy-start(f32[16,512]{1,0:T(8,128)} %param.11) | copy-start | bytes 98308
  658.2 28.9 %slice-start = ((s8[12582912]{0:T(1024)(128)(4,1)}), s8[4194304]{0:T(1024)(128)(4,1)S(1)}, s32[]{:S(2)}) async-start(s8[12582912]{0:T(1024)(128)(4,1)} %bitcast.40), calls=%async_computation.2 | async-start | bytes 8388608
  658.2 28.9 %slice-start.1 = ((s8[12582912]{0:T(1024)(128)(4,1)}), s8[4194304]{0:T(1024)(128)(4,1)S(1)}, s32[]{:S(2)}) async-start(s8[12582912]{0:T(1024)(128)(4,1)} %bitcast.40), calls=%async_computation.3 | async-start | bytes 8388608
  668.8 18.3 %slice-start.2 = ((s8[12582912]{0:T(1024)(128)(4,1)}), s8[4194304]{0:T(1024)(128)(4,1)S(1)}, s32[]{:S(2)}) async-start(s8[12582912]{0:T(1024)(128)(4,1)} %bitcast.40), calls=%async_computation.4 | async-start | bytes 8388608
  687.1 17.8 %copy-start.5 = (f32[768]{0:T(1024)S(1)}, f32[768]{0:T(1024)}, u32[]{:S(2)}) copy-start(f32[768]{0:T(1024)} %param.13) | copy-start | bytes 9220
  705.0 19.5 %copy-start.3 = (bf16[768,768]{1,0:T(8,128)(2,1)S(1)}, bf16[768,768]{1,0:T(8,128)(2,1)}, u32[]{:S(2)}) copy-start(bf16[768,768]{1,0:T(8,128)(2,1)} %param.15) | copy-start | bytes 3538948
  724.4 33.6 %copy-start.1 = (bf16[768,768]{1,0:T(8,128)(2,1)S(1)}, bf16[768,768]{1,0:T(8,128)(2,1)}, u32[]{:S(2)}) copy-start(bf16[768,768]{1,0:T(8,128)(2,1)} %param.14) | copy-start | bytes 3538948
where the time goes:
time: 760 us; the launch traced here: 758 us
  blocking collectives  557 us (73%)
  matrix products  87.2 us (11%)
  local copies, waits for them, and re-layouts  66.6 us (9%)
  other arithmetic  47.4 us (6%)
    all_to_all x1, blocking collectives, body(): lax.all_to_all(section_one, 'seq', split_axis=2, concat_axis=1, tiled=True)  279 us
    all_to_all x1, blocking collectives, body(): lax.all_to_all(mixed_cols, 'seq', split_axis=1, concat_axis=2, tiled=True)  278 us
    dot_general x1, matrix products, body(): gates = jnp.dot(mix_normed, gate_weight, preferred_element_type=jnp.float32)  33.6 us
    reduce_sum x2, other arithmetic, rms_scale(): mean_square = jnp.mean(values * values, axis=-1, keepdims=True)  25 us
    dot_general x1, matrix products, body(): jnp.dot(mix_normed, value_weight, preferred_element_type=jnp.float32)  19.5 us
    convert_element_type x1, local copies, waits for them, and re-layouts, body(): mixed_back.reshape(seqs_here, rows_here, width).astype(jnp.float32)  18.3 us
    dot_general x1, matrix products, second_section(): jnp.einsum('jia,sajc->sijc', left_factor, columns, preferred_element_type...  18.1 us
    convert_element_type x1, local copies, waits for them, and re-layouts, body(): section_one = (section_one * twiddle[None, :, :, None]).astype(jnp.bfloat16)  17.6 us

commit v1 on v0

--- a/solution.py
+++ b/solution.py
@@ -1,7 +1,280 @@
+import functools
+
 import jax
 import jax.numpy as jnp
 from jax import lax
+from jax.experimental import pallas as pl
+from jax.experimental.pallas import tpu as pltpu
 from jax.sharding import PartitionSpec as P
+
+MESH = pl.DeviceIdType.MESH
+T = 16
+GROUP = 2
+HALVES = 2
+
+
+def layer_kernel(
+    n,
+    tok_hbm, right_hbm, left_hbm, tw_ref, ngain_ref, mgain_ref, wv_hbm, wg_hbm,
+    out_hbm,
+    sbuf, r1, r2, tbuf, rbuf, nbuf, twt, lbuf, wv, wg, perm, kbuf, obuf,
+    send1, recv1, send2, recv2, tsem, rsem, wsem, ksem, osem,
+):
+    me = lax.axis_index("seq")
+    grp = lax.axis_index("grp")
+    block_len = tbuf.shape[1]
+    width = tbuf.shape[2]
+
+    def load_block(a, slot):
+        return (
+            pltpu.make_async_copy(tok_hbm.at[a], tbuf.at[slot], tsem.at[slot]),
+            pltpu.make_async_copy(right_hbm.at[a], rbuf.at[slot], rsem.at[slot]),
+        )
+
+    for copy in load_block(0, 0):
+        copy.start()
+    weights = [
+        pltpu.make_async_copy(left_hbm, lbuf, wsem.at[0]),
+        pltpu.make_async_copy(wv_hbm, wv, wsem.at[1]),
+        pltpu.make_async_copy(wg_hbm, wg, wsem.at[2]),
+    ]
+
+    barrier = pltpu.get_barrier_semaphore()
+
+    @pl.loop(1, n)
+    def _(k):
+        pl.semaphore_signal(
+            barrier, inc=1, device_id=(grp, lax.rem(me + k, n)), device_id_type=MESH
+        )
+
+    row = lax.broadcasted_iota(jnp.int32, (T * T, T * T), 0)
+    col = lax.broadcasted_iota(jnp.int32, (T * T, T * T), 1)
+    swapped = (row % T) * T + row // T
+    perm[...] = jnp.where(col == swapped, 1.0, 0.0).astype(jnp.bfloat16)
+    twt[...] = tw_ref[...].T
+    pl.semaphore_wait(barrier, n - 1)
+
+    def first(a):
+        slot = lax.rem(a, 2)
+        for copy in load_block(a, slot):
+            copy.wait()
+
+        @pl.when(a + 1 < T)
+        def _():
+            for copy in load_block(a + 1, 1 - slot):
+                copy.start()
+
+        chunk = 64
+
+        @pl.loop(0, block_len // chunk)
+        def _(q):
+            rows = pl.ds(pl.multiple_of(q * chunk, chunk), chunk)
+            x = tbuf[slot, rows, :].astype(jnp.float32)
+            scale = lax.rsqrt(jnp.mean(x * x, axis=-1, keepdims=True) + 1e-05)
+            nbuf[rows, :] = (x * scale * ngain_ref[...]).astype(jnp.bfloat16)
+
+        part = 256
+        for q in range(block_len // part):
+            rows = pl.ds(q * part, part)
+            tw = twt[rows, :]
+            lane = lax.broadcasted_iota(jnp.int32, tw.shape, 1)
+            tw = jnp.sum(jnp.where(lane == a, tw, 0.0), axis=1, keepdims=True)
+            s1 = jnp.dot(rbuf[slot, rows, :], nbuf[...], preferred_element_type=jnp.float32)
+            s1 = (s1 * tw).astype(jnp.bfloat16).reshape(part // (T * HALVES), HALVES, T, width)
+            for d in range(s1.shape[0]):
+                for h in range(HALVES):
+                    sbuf[h, q * s1.shape[0] + d, a] = s1[d, h]
+
+    def send_first(h, k, a0, count):
+        d = lax.rem(me + k, n)
+        blocks = pl.ds(a0, count)
+        pltpu.make_async_remote_copy(
+            src_ref=sbuf.at[h, d, blocks],
+            dst_ref=r1.at[h, me, blocks],
+            send_sem=send1.at[h, k],
+            recv_sem=recv1.at[h, me],
+            device_id=(grp, d),
+            device_id_type=MESH,
+        ).start()
+
+    @pl.loop(0, T // GROUP)
+    def _(g):
+        @pl.loop(0, GROUP)
+        def _(u):
+            first(g * GROUP + u)
+
+        @pl.loop(1, n)
+        def _(k):
+            send_first(0, k, g * GROUP, GROUP)
+
+        @pl.when(g == 0)
+        def _():
+            for copy in weights:
+                copy.start()
+
+    @pl.loop(1, HALVES)
+    def _(h):
+        @pl.loop(1, n)
+        def _(k):
+            send_first(h, k, 0, T)
+
+    @pl.loop(0, HALVES)
+    def _(h):
+        pltpu.make_async_copy(sbuf.at[h, me], r1.at[h, me], recv1.at[h, me]).start()
+
+    for copy in weights:
+        copy.wait()
+
+    @pl.loop(0, HALVES)
+    def _(h):
+        @pl.loop(0, n)
+        def _(k):
+            s = lax.rem(me + n - k, n)
+            tile = r1.at[h, s]
+            pltpu.make_async_copy(tile, tile, recv1.at[h, s]).wait()
+            x = jnp.dot(
+                perm[...], r1[h, s].reshape(T * T, width), preferred_element_type=jnp.float32
+            )
+            r1[h, s] = x.astype(jnp.bfloat16).reshape(T, T, width)
+
+        @pl.loop(1, n)
+        def _(k):
+            tile = sbuf.at[h, 0]
+            pltpu.make_async_copy(tile, tile, send1.at[h, k]).wait()
+
+        @pl.loop(0, T)
+        def _(j):
+            x = r1[h, :, j].reshape(n * T, width)
+            mixed = jnp.dot(lbuf[h * T + j], x, preferred_element_type=jnp.float32)
+            sbuf[h, :, j] = mixed.astype(jnp.bfloat16).reshape(n, T, width)
+
+        @pl.loop(1, n)
+        def _(k):
+            d = lax.rem(me + k, n)
+            pltpu.make_async_remote_copy(
+                src_ref=sbuf.at[h, d],
+                dst_ref=r2.at[h, me],
+                send_sem=send2.at[h, k],
+                recv_sem=recv2.at[h, me],
+                device_id=(grp, d),
+                device_id_type=MESH,
+            ).start()
+
+        pltpu.make_async_copy(sbuf.at[h, me], r2.at[h, me], recv2.at[h, me]).start()
+
+    def columns(t):
+        h = t // n
+        s = lax.rem(me + n - lax.rem(t, n), n)
+        return h, s, pl.ds(pl.multiple_of((s * HALVES + h) * T, T), T)
+
+    def load_tokens(t, slot):
+        _, _, cols = columns(t)
+        return pltpu.make_async_copy(tok_hbm.at[:, cols], kbuf.at[slot], ksem.at[slot])
+
+    def store_out(t, slot):
+        _, _, cols = columns(t)
+        return pltpu.make_async_copy(obuf.at[slot], out_hbm.at[:, cols], osem.at[slot])
+
+    load_tokens(0, 0).start()
+    tiles = HALVES * n
+
+    @pl.loop(0, tiles)
+    def _(t):
+        slot = lax.rem(t, 2)
+        h, s, _ = columns(t)
+        load_tokens(t, slot).wait()
+
+        @pl.when(t + 1 < tiles)
+        def _():
+            load_tokens(t + 1, 1 - slot).start()
+
+        tile = r2.at[h, s]
+        pltpu.make_async_copy(tile, tile, recv2.at[h, s]).wait()
+        mixed = jnp.dot(
+            perm[...], r2[h, s].reshape(T * T, width), preferred_element_type=jnp.float32
+        )
+        res = kbuf[slot].reshape(T * T, width).astype(jnp.float32) + mixed
+        scale = lax.rsqrt(jnp.mean(res * res, axis=-1, keepdims=True) + 1e-05)
+        normed = (res * scale * mgain_ref[...]).astype(jnp.bfloat16)
+
+        @pl.when(t >= 2)
+        def _():
+            store_out(t - 2, slot).wait()
+
+        step = 256
+        for c in range(0, width, step):
+            cols = slice(c, c + step)
+            v = jnp.dot(normed, wv[:, cols], preferred_element_type=jnp.float32)
+            g = jnp.dot(normed, wg[:, cols], preferred_element_type=jnp.float32)
+            out = res[:, cols] + v * jax.nn.sigmoid(g)
+            obuf[slot, :, :, cols] = out.astype(jnp.bfloat16).reshape(T, T, step)
+        store_out(t, slot).start()
+
+    for t in (tiles - 2, tiles - 1):
+        store_out(t, t % 2).wait()
+
+    @pl.loop(0, HALVES)
+    def _(h):
+        @pl.loop(1, n)
+        def _(k):
+            tile = sbuf.at[h, 0]
+            pltpu.make_async_copy(tile, tile, send2.at[h, k]).wait()
+
+
+def fused_body(
+    n, tokens, right_factor, left_factor, twiddle, norm_gain, mix_gain, value_weight, gate_weight
+):
+    _, rows_here, width = tokens.shape
+    block_len = right_factor.shape[1]
+    order = left_factor.shape[1]
+    bf16, f32 = jnp.bfloat16, jnp.float32
+    hbm = pl.BlockSpec(memory_space=pl.ANY)
+    vmem = pl.BlockSpec(memory_space=pltpu.VMEM)
+    dma = pltpu.SemaphoreType.DMA
+    exchange = pltpu.VMEM((HALVES, n, T, T, width), bf16)
+    out = pl.pallas_call(
+        functools.partial(layer_kernel, n),
+        out_shape=jax.ShapeDtypeStruct((T, block_len, width), bf16),
+        in_specs=[hbm, hbm, hbm, vmem, vmem, vmem, hbm, hbm],
+        out_specs=hbm,
+        scratch_shapes=[
+            exchange,
+            exchange,
+            exchange,
+            pltpu.VMEM((2, block_len, width), bf16),
+            pltpu.VMEM((2, block_len, block_len), bf16),
+            pltpu.VMEM((block_len, width), bf16),
+            pltpu.VMEM((block_len, T), f32),
+            pltpu.VMEM((HALVES * T, order, order), bf16),
+            pltpu.VMEM((width, width), bf16),
+            pltpu.VMEM((width, width), bf16),
+            pltpu.VMEM((T * T, T * T), bf16),
+            pltpu.VMEM((2, T, T, width), bf16),
+            pltpu.VMEM((2, T, T, width), bf16),
+            dma((HALVES, n)),
+            dma((HALVES, n)),
+            dma((HALVES, n)),
+            dma((HALVES, n)),
+            dma((2,)),
+            dma((2,)),
+            dma((3,)),
+            dma((2,)),
+            dma((2,)),
+        ],
+        compiler_params=pltpu.CompilerParams(
+            collective_id=0, has_side_effects=True, vmem_limit_bytes=58 * 2**20
+        ),
+    )(
+        tokens.reshape(T, block_len, width),
+        right_factor,
+        left_factor,
+        twiddle,
+        norm_gain.reshape(1, width),
+        mix_gain.reshape(1, width),
+        value_weight,
+        gate_weight,
+    )
+    return out.reshape(tokens.shape)
 
 
 def rms_scale(values, gain):
@@ -20,6 +293,11 @@
     seqs_here, rows_here, width = tokens.shape
     blocks_here = right_factor.shape[0]
     block_len = right_factor.shape[1]
+    n = lax.axis_size("seq")
+    if seqs_here == 1 and blocks_here == T and n * T == left_factor.shape[1] and n * T * HALVES == block_len:
+        return fused_body(
+            n, tokens, right_factor, left_factor, twiddle, norm_gain, mix_gain, value_weight, gate_weight
+        )
     widened = tokens.astype(jnp.float32)
     normed = rms_scale(widened, norm_gain).astype(jnp.bfloat16)
     blocked = normed.reshape(seqs_here, blocks_here, block_len, width)

time: 760 us -> 578 us (0.76)
  Pallas kernels: 0 us -> 565 us
  blocking collectives: 557 us -> 0 us
  matrix products: 87.2 us -> 0 us
  local copies, waits for them, and re-layouts: 66.6 us -> 13 us
  other arithmetic: 47.4 us -> 0 us
    pallas_call x0 -> x1, Pallas kernels: none -> 565 us  [fused_body(): pl.pallas_call(functools.partial(layer_kernel, n), out_shape=jax.ShapeDty...]
    all_to_all x2 -> x0, blocking collectives: 557 us -> none  [the longest x1 279 us: body(): lax.all_to_all(section_one, 'seq', split_axis=2, concat_axis=1, tiled=True)]
    dot_general x4 -> x0, matrix products: 87.2 us -> none  [the longest x1 33.6 us: body(): gates = jnp.dot(mix_normed, gate_weight, preferred_element_type=jnp.float32)]
    convert_element_type x3 -> x0, local copies, waits for them, and re-layouts: 52.4 us -> none  [the longest x1 18.3 us: body(): mixed_back.reshape(seqs_here, rows_here, width).astype(jnp.float32)]
    reduce_sum x2 -> x0, other arithmetic: 25 us -> none  [rms_scale(): mean_square = jnp.mean(values * values, axis=-1, keepdims=True)]
    convert_element_type x2 -> x0, other arithmetic: 22.4 us -> none  [the longest x1 11.8 us: body(): normed = rms_scale(widened, norm_gain).astype(jnp.bfloat16)]
    all_to_all x2 -> x0, local copies, waits for them, and re-layouts: 14.2 us -> none  [body(): lax.all_to_all(section_one, 'seq', split_axis=2, concat_axis=1, tiled=True)]
    unnamed x18 -> x1, local copies, waits for them, and re-layouts: 0.04 us -> 10.5 us
where the time goes in v1:
time: 578 us
  Pallas kernels  565 us (98%)
  local copies, waits for them, and re-layouts  13 us (2%)
    pallas_call x1, Pallas kernels, fused_body(): pl.pallas_call(functools.partial(layer_kernel, n), out_shape=jax.ShapeDty...  565 us

profile of v1, /device:TPU:13, one launch (start us, length us, event | category | flops | bytes accessed | tf_op | source)
XLA Modules:
  0.0 577.8 jit_solution(4801608394859011708)
XLA Ops:
  0.0 1.3 reshape.13.ngain_ref
  1.3 1.3 reshape.14.mgain_ref
  2.5 564.8 %shard_map.82 = bf16[16,512,768]{2,1,0:T(8,128)(2,1)} custom-call(bf16[16,512,768]{2,1,0:T(8,128)(2,1)} %bitcast.3, bf16[16,512,512]{2,1,0:T(8,128)(2,1)} %right_hbm.1, bf16[32,256,256]{2,1,0:T(8,128)(2,1)} %left_hbm.1, f32[16,512]{1,0:T(8,128)} %tw_ref.1, f32[1,768]{1,0:T(1,128)} %reshape.13.ngain_ref, f32[1,768]{1,0:T(1,128)} %reshape.14.mgain_ref, ...), custom_call_target="tpu_custom_call" | custom-call | tf_op jit(solution)/shard_map/pallas_call | solution.py:235
  567.4 10.5 %copy.10 = bf16[1,8192,768]{2,1,0:T(8,128)(2,1)} copy(bf16[1,8192,768]{2,1,0:T(8,128)(2,1)} %bitcast.2) | data formatting | bytes 25165824

commit v2 on v1

--- a/solution.py
+++ b/solution.py
@@ -71,7 +71,7 @@
             rows = pl.ds(pl.multiple_of(q * chunk, chunk), chunk)
             x = tbuf[slot, rows, :].astype(jnp.float32)
             scale = lax.rsqrt(jnp.mean(x * x, axis=-1, keepdims=True) + 1e-05)
-            nbuf[rows, :] = (x * scale * ngain_ref[...]).astype(jnp.bfloat16)
+            nbuf[rows, :] = (x * scale * ngain_ref[...].reshape(1, width)).astype(jnp.bfloat16)
 
         part = 256
         for q in range(block_len // part):
@@ -195,7 +195,7 @@
         )
         res = kbuf[slot].reshape(T * T, width).astype(jnp.float32) + mixed
         scale = lax.rsqrt(jnp.mean(res * res, axis=-1, keepdims=True) + 1e-05)
-        normed = (res * scale * mgain_ref[...]).astype(jnp.bfloat16)
+        normed = (res * scale * mgain_ref[...].reshape(1, width)).astype(jnp.bfloat16)
 
         @pl.when(t >= 2)
         def _():
@@ -269,8 +269,8 @@
         right_factor,
         left_factor,
         twiddle,
-        norm_gain.reshape(1, width),
-        mix_gain.reshape(1, width),
+        norm_gain,
+        mix_gain,
         value_weight,
         gate_weight,
     )

time: 578 us -> 576 us (level)
  no operation moved by 1% of the time
where the time goes in v2:
time: 576 us; the launch traced here: 575 us
  Pallas kernels  565 us (98%)
  local copies, waits for them, and re-layouts  10.5 us (2%)
    pallas_call x1, Pallas kernels, fused_body(): pl.pallas_call(functools.partial(layer_kernel, n), out_shape=jax.ShapeDty...  565 us

profile of v2, /device:TPU:13, one launch (start us, length us, event | category | flops | bytes accessed | tf_op | source)
XLA Modules:
  0.0 575.3 jit_solution(9191798880758577222)
XLA Ops:
  0.0 564.8 %shard_map.82 = bf16[16,512,768]{2,1,0:T(8,128)(2,1)} custom-call(bf16[16,512,768]{2,1,0:T(8,128)(2,1)} %bitcast.3, bf16[16,512,512]{2,1,0:T(8,128)(2,1)} %right_hbm.1, bf16[32,256,256]{2,1,0:T(8,128)(2,1)} %left_hbm.1, f32[16,512]{1,0:T(8,128)} %tw_ref.1, f32[768]{0:T(1024)} %ngain_ref.1, f32[768]{0:T(1024)} %mgain_ref.1, bf16[768,768]{1,0:T(8,128)(2,1)} %wv_hbm.1, ...), custom_call_target="tpu_custom_call" | custom-call | tf_op jit(solution)/shard_map/pallas_call | solution.py:235
  564.8 10.5 %copy.10 = bf16[1,8192,768]{2,1,0:T(8,128)(2,1)} copy(bf16[1,8192,768]{2,1,0:T(8,128)(2,1)} %bitcast.2) | data formatting | bytes 25165824
